TPU v7x, 32 devices: a whole 2x2x4 slice. The times are simulated.
32 devices in a mesh: scene: 2 (over x), gx: 16 (over z, y, core).
Axes of the slice: x: 2, y: 2, z: 4, core: 2. Of those that a mesh axis runs over, the one named last changes fastest.
Arguments:
- feats: bfloat16 [128, 64, 256], P(('scene', 'gx')), parts along dimension 0, may hold values from -6 to 6
- voxel_mask: int32 [128, 64], P(('scene', 'gx')), parts along dimension 0, may hold values 0 or 1
- brick_table: int32 [128, 27], P(('scene', 'gx')), parts along dimension 0, may hold values from 0 to 12, as said below
- counts: int32 [32], P(('scene', 'gx')), parts along dimension 0, may hold values from 1 to 4, as said below
- weight_one: bfloat16 [6912, 256], replicated, may hold values from -0.078125 to 0.078125
- weight_two: bfloat16 [6912, 256], replicated, may hold values from -0.078125 to 0.078125
- cotangent: bfloat16 [128, 64, 256], P(('scene', 'gx')), parts along dimension 0, may hold values from -6 to 6
Outputs:
- block_out: bfloat16 [128, 64, 256], P(('scene', 'gx')), parts along dimension 0
- feats_grad: bfloat16 [128, 64, 256], P(('scene', 'gx')), parts along dimension 0
- grad_one: float32 [13824, 256], P(('scene', 'gx')), parts along dimension 0
There are 2 independent parts, one for each index of `scene`. A program takes and returns all parts, laid end to end along the dimension named above; an argument that names none is the same for every part. Nothing has to cross between parts.
Inputs may be any that keep to these rules, and one draw needn't show every extreme that they name: `counts`: every owner has between 4 // 4 (at least 1) and 4 active bricks; both ends are taken by some owner in every draw. `brick_table`: entry q = 9 (dx + 1) + 3 (dy + 1) + (dz + 1). Values below 4 (the left owner's slots) appear only where dx = -1 and values from 8 to 3 * 4 - 1 (the right owner's) only where dx = +1; they name only active slots, and the first owner never names a left slot, the last never a right one. Entry 13 of an active slot is 4 plus the slot itself; 12 means no neighbour; inactive slots hold 12 everywhere and are never named.
All inputs are finite; a program needn't handle non-finite values. No bound on the sum of `voxel_mask` on one device may be relied on, other than what follows from the above.
Results may differ from a plain program's by a relative error of at most 0.0029.
Values may be sent and summed in bfloat16 or wider, within the bound.
A program may use at most 128 MiB of HBM per device.

v0:
```python
import jax
import jax.numpy as jnp
from jax import lax
from jax.experimental import pallas as pl
from jax.experimental.pallas import tpu as pltpu
from jax.sharding import PartitionSpec as P

F32, BF16 = jnp.float32, jnp.bfloat16
VMEM = pl.BlockSpec(memory_space=pltpu.VMEM)
SMEM = pl.BlockSpec(memory_space=pltpu.SMEM)

ROWS, SIDE = 256, 16


def iota(shape, dim):
    return lax.broadcasted_iota(jnp.int32, shape, dim)


def natural_of(row):
    return ((row >> 2) & 3) * 64 + (row >> 6) * 16 + ((row >> 4) & 3) * 4 + (row & 3)


def to_rows():
    shape = (ROWS, ROWS)
    return (natural_of(iota(shape, 0)) == iota(shape, 1)).astype(F32).astype(BF16)


def from_rows():
    shape = (ROWS, ROWS)
    return (natural_of(iota(shape, 1)) == iota(shape, 0)).astype(F32).astype(BF16)


def mat(a, b):
    return jnp.dot(a, b, preferred_element_type=F32)


def mask_rows(mask_ref, counts_ref):
    row = iota((ROWS, 64), 0)
    brick = (row >> 2) & 3
    held = mask_ref[...].astype(F32)
    spread = jnp.zeros((ROWS, 64), F32)
    for b in range(4):
        spread = jnp.where(brick == b, held[b : b + 1, :], spread)
    keep = (iota((ROWS, 64), 1) == (natural_of(row) & 63)) & (brick < counts_ref[0])
    return jnp.sum(jnp.where(keep, spread, 0.0), axis=1, keepdims=True)


def pickers(table_ref):
    row = iota((128, 27), 0) & 63
    shift, brick, k = row >> 4, (row >> 2) & 3, row & 3
    moved = k + shift - 1
    step = jnp.where(moved < 0, 0, jnp.where(moved > 3, 2, 1))
    held = table_ref[...].astype(F32)
    spread = jnp.zeros((128, 27), F32)
    for b in range(4):
        spread = jnp.where(brick == b, held[b : b + 1, :], spread)
    lane = iota((128, 128), 1)
    wide = iota((128, 128), 0) & 63
    source = ((wide & 3) + (wide >> 4) - 1) & 3
    fits = ((lane & 3) == source) & (wide < 48)
    picks = {}
    for qa in range(3):
        for qb in range(3):
            chosen = iota((128, 27), 1) == qa * 9 + qb * 3 + step
            entry = jnp.sum(jnp.where(chosen, spread, 0.0), axis=1, keepdims=True)
            hit = fits & (entry.astype(jnp.int32) == (lane >> 2)) & (lane < 48)
            picks[qa, qb] = hit.astype(F32)
    return picks


def places():
    for wi in range(6):
        for wj in range(6):
            qa, qb = (wi + 3) // 4, (wj + 3) // 4
            yield wi, wj, (qa, qb), (wi + 3) % 4, (wj + 3) % 4


def gather_windows(picks, lower, own, upper, win):
    half = {key: value[:48, :48].astype(BF16) for key, value in picks.items()}
    for wi, wj, q, i, j in places():
        at = pl.ds((i * 4 + j) * SIDE, SIDE)
        source = jnp.concatenate([lower[at], own[at], upper[at]], 0)
        got = mat(half[q], source).astype(BF16)
        for c in range(3):
            win[c, wi, wj] = got[c * SIDE : (c + 1) * SIDE]


def build_stack(win, stack):
    for o in range(27):
        a, b, c = o // 9, o // 3 % 3, o % 3
        stack[:, o * 256 : (o + 1) * 256] = win[c, a : a + 4, b : b + 4].reshape(ROWS, 256)


def spread_back(picks, grad, weight_ref, acc, own, lower, upper):
    acc[...] = jnp.zeros(acc.shape, F32)
    for o in range(27):
        a, b, c = o // 9, o // 3 % 3, o % 3
        part = lax.dot_general(
            grad,
            weight_ref[o * 256 : (o + 1) * 256, :],
            (((1,), (1,)), ((), ())),
            preferred_element_type=F32,
        )
        acc[c, a : a + 4, b : b + 4] += part.reshape(4, 4, SIDE, 256)
    turned = {key: value.T[:48].astype(BF16) for key, value in picks.items()}
    pad = jnp.zeros((SIDE, 256), BF16)
    totals = {}
    for wi, wj, q, i, j in places():
        held = acc[:, wi, wj].reshape(48, 256)
        high = held.astype(BF16)
        low = (held - high.astype(F32)).astype(BF16)
        got = mat(turned[q], jnp.concatenate([high, pad, low, pad], 0))
        totals[i, j] = totals[i, j] + got if (i, j) in totals else got
    for (i, j), value in totals.items():
        at = pl.ds((i * 4 + j) * SIDE, SIDE)
        lower[at] = value[:16].astype(BF16)
        own[at] = value[16:32]
        upper[at] = value[32:48].astype(BF16)


def first_kernel(feats, cot, mask, table, counts, w2, x0, g2, own, lower, upper, acc):
    keep = mask_rows(mask, counts)
    turn = to_rows()
    x0[...] = (mat(turn, feats[...]) * keep).astype(BF16)
    grad = (mat(turn, cot[...]) * keep).astype(BF16)
    g2[...] = grad
    spread_back(pickers(table), grad, w2, acc, own, lower, upper)


def second_kernel(
    x0_low, x0, x0_up, d_own, d_up, d_low, mask, table, counts, w1,
    a1, own, lower, upper, grad_w, win, stack, acc,
):
    keep = mask_rows(mask, counts)
    picks = pickers(table)
    gather_windows(picks, x0_low, x0, x0_up, win)
    build_stack(win, stack)
    y1 = mat(stack[...], w1[...]) * keep
    sig = 1.0 / (1.0 + jnp.exp(-y1))
    a1[...] = (y1 * sig).astype(BF16)
    da1 = d_own[...] + d_up[...].astype(F32) + d_low[...].astype(F32)
    g1 = (da1 * keep * (sig * (1.0 + y1 * (1.0 - sig)))).astype(BF16)
    for o in range(27):
        at = slice(o * 256, (o + 1) * 256)
        grad_w[at, :] = lax.dot_general(
            stack[:, at], g1, (((0,), (0,)), ((), ())), preferred_element_type=F32
        )
    spread_back(picks, g1, w1, acc, own, lower, upper)


def third_kernel(
    a_low, a1, a_up, f_own, f_up, f_low, x0, g2, mask, table, counts, w2,
    block_out, feats_grad, win, stack,
):
    keep = mask_rows(mask, counts)
    gather_windows(pickers(table), a_low, a1, a_up, win)
    build_stack(win, stack)
    y2 = mat(stack[...], w2[...]) * keep
    out = (y2 + x0[...].astype(F32)).astype(BF16)
    turn = from_rows()
    block_out[...] = mat(turn, out).astype(BF16)
    total = f_own[...] + f_up[...].astype(F32) + f_low[...].astype(F32)
    grad = (keep * (total + g2[...].astype(F32))).astype(BF16)
    feats_grad[...] = mat(turn, grad).astype(BF16)


def rows_of(kind):
    return jax.ShapeDtypeStruct((ROWS, 256), kind)


PARAMS = pltpu.CompilerParams(vmem_limit_bytes=50 * 2**20)
WIN = pltpu.VMEM((3, 6, 6, SIDE, 256), BF16)
ACC = pltpu.VMEM((3, 6, 6, SIDE, 256), F32)
STACK = pltpu.VMEM((ROWS, 6912), BF16)


def shifted(value, steps):
    count = lax.axis_size("gx")
    first, last = (max(0, -steps), min(count, count - steps))
    return lax.ppermute(value, "gx", [(source, source + steps) for source in range(first, last)])


def exchange(field, lower, upper):
    up = shifted(jnp.concatenate([field, upper], 0), 1)
    down = shifted(jnp.concatenate([field, lower], 0), -1)
    return up[:ROWS], down[:ROWS], up[ROWS:], down[ROWS:]


def on_device(feats, voxel_mask, brick_table, counts, weight_one, weight_two, cotangent):
    per, vb, ch = feats.shape
    kc = weight_one.shape[0]
    small = (voxel_mask, brick_table, counts)
    small_specs = [VMEM, VMEM, SMEM]
    x0, g2, d_own, d_lower, d_upper = pl.pallas_call(
        first_kernel,
        out_shape=[rows_of(BF16), rows_of(BF16), rows_of(F32), rows_of(BF16), rows_of(BF16)],
        in_specs=[VMEM, VMEM, *small_specs, VMEM],
        out_specs=[VMEM] * 5,
        scratch_shapes=[ACC],
        compiler_params=PARAMS,
    )(feats.reshape(per * vb, ch), cotangent.reshape(per * vb, ch), *small, weight_two)
    x_low, x_up, d_low, d_up = exchange(x0, d_lower, d_upper)
    a1, f_own, f_lower, f_upper, grad_w = pl.pallas_call(
        second_kernel,
        out_shape=[
            rows_of(BF16), rows_of(F32), rows_of(BF16), rows_of(BF16),
            jax.ShapeDtypeStruct((kc, ch), F32),
        ],
        in_specs=[VMEM] * 6 + small_specs + [VMEM],
        out_specs=[VMEM] * 5,
        scratch_shapes=[WIN, STACK, ACC],
        compiler_params=PARAMS,
    )(x_low, x0, x_up, d_own, d_up, d_low, *small, weight_one)
    grad_one = lax.psum_scatter(grad_w, "gx", scatter_dimension=0, tiled=True)
    a_low, a_up, f_low, f_up = exchange(a1, f_lower, f_upper)
    block_out, feats_grad = pl.pallas_call(
        third_kernel,
        out_shape=[rows_of(BF16), rows_of(BF16)],
        in_specs=[VMEM] * 8 + small_specs + [VMEM],
        out_specs=[VMEM] * 2,
        scratch_shapes=[WIN, STACK],
        compiler_params=PARAMS,
    )(a_low, a1, a_up, f_own, f_up, f_low, x0, g2, *small, weight_two)
    return (block_out.reshape(per, vb, ch), feats_grad.reshape(per, vb, ch), grad_one)


def solution(mesh):
    split = ("scene", "gx")
    in_specs = (
        P(split, None, None), P(split, None), P(split, None), P(split), P(), P(),
        P(split, None, None),
    )
    out_specs = (P(split, None, None), P(split, None, None), P(split, None))
    return jax.shard_map(
        on_device, mesh=mesh, in_specs=in_specs, out_specs=out_specs, check_vma=False
    )
```

profile of v0, /device:TPU:0, one launch (start us, length us, event | category | flops | bytes accessed | tf_op | source)
XLA Modules:
  0.0 134.5 jit_solution(5889410853330028778)
XLA Ops:
  7.2 0.0 copy-start.5
  7.2 0.0 reduce-scatter.2.cloned.1.call-start
  7.9 0.0 copy-start
  7.9 0.9 copy-done
  8.8 0.0 copy-start.1
  8.8 0.9 copy-done.1
  9.7 0.0 copy-start.2
  9.7 0.7 copy-done.2
  10.4 0.7 copy-done.4
  11.0 4.0 %shard_map.94 = (bf16[256,256]{1,0:T(8,128)(2,1)S(1)}, bf16[256,256]{1,0:T(8,128)(2,1)S(1)}, f32[256,256]{1,0:T(8,128)S(1)}, bf16[256,256]{1,0:T(8,128)(2,1)S(1)}, bf16[256,256]{1,0:T(8,128)(2,1)S(1)}) custom-call(bf16[256,256]{1,0:T(8,128)(2,1)S(1)} %bitcast.4, bf16[256,256]{1,0:T(8,128)(2,1)S(1)} %bitcast.5, s32[4,64]{1,0:T(4,128)S(1)} %copy-done.2, ...), custom_call_target="tpu_custom_call" | custom-call | tf_op jit(solution)/shard_map/pallas_call | solution.py:194
  15.1 1.3 collective-permute-start.1
  16.4 3.0 %collective-permute-start = (bf16[512,256]{1,0:T(8,128)(2,1)S(1)}, bf16[512,256]{1,0:T(8,128)(2,1)S(1)}, u32[]{:S(2)}, u32[]{:S(2)}) collective-permute-start(bf16[512,256]{1,0:T(8,128)(2,1)S(1)} %get-tuple-element.38), channel_id=1, source_target_pairs={{0,1},{1,2},{2,3},{3,4},{4,5},{5,6},{6,7},{7,8},{8,9},{9,10},{10,1... | collective-permute-start | bytes 786440 | tf_op jit(solution)/shard_map/ppermute | solution.py:180
  19.5 0.0 collective-permute-done.1
  19.5 1.1 collective-permute-done
  20.6 0.0 copy-done.5
  20.6 9.2 %shard_map.95 = (bf16[256,256]{1,0:T(8,128)(2,1)S(1)}, f32[256,256]{1,0:T(8,128)S(1)}, bf16[256,256]{1,0:T(8,128)(2,1)S(1)}, bf16[256,256]{1,0:T(8,128)(2,1)S(1)}, f32[6912,256]{1,0:T(8,128)}) custom-call(bf16[256,256]{1,0:T(8,128)(2,1)S(1)} %get-tuple-element.32.x0_low, bf16[256,256]{1,0:T(8,128)(2,1)S(1)} %get-tuple-element.15.x0, ...), custom_call_target="tpu_custom_call" | custom-call | tf_op jit(solution)/shard_map/pallas_call | solution.py:203
  29.8 0.0 reduce-scatter.2.cloned.1.call-update
  29.9 1.3 collective-permute-start.3
  31.2 9.1 %collective-permute-start.2 = (bf16[512,256]{1,0:T(8,128)(2,1)S(1)}, bf16[512,256]{1,0:T(8,128)(2,1)S(1)}, u32[]{:S(2)}, u32[]{:S(2)}) collective-permute-start(bf16[512,256]{1,0:T(8,128)(2,1)S(1)} %get-tuple-element.36), channel_id=1, source_target_pairs={{0,1},{1,2},{2,3},{3,4},{4,5},{5,6},{6,7},{7,8},{8,9},{9,10},{10,1... | collective-permute-start | bytes 786440 | tf_op jit(solution)/shard_map/ppermute | solution.py:180
  40.3 0.0 collective-permute-done.3
  40.3 1.1 collective-permute-done.2
  41.4 0.0 copy-done.3
  41.4 4.7 %shard_map.96 = (bf16[256,256]{1,0:T(8,128)(2,1)}, bf16[256,256]{1,0:T(8,128)(2,1)}) custom-call(bf16[256,256]{1,0:T(8,128)(2,1)S(1)} %get-tuple-element.28.a_low, bf16[256,256]{1,0:T(8,128)(2,1)S(1)} %get-tuple-element.19.a1, bf16[256,256]{1,0:T(8,128)(2,1)S(1)} %get-tuple-element.30.a_up, f32[256,256]{1,0:T(8,128)S(1)} %get-tuple-element.22.f_own, ...), custom_call_target="tpu_custom_call" | custom-call | tf_op jit(solution)/shard_map/pallas_call | solution.py:216
  46.1 81.5 %reduce-scatter.2.cloned.1.call-done = f32[432,256]{1,0:T(8,128)} async-done(((f32[6912,256]{1,0:T(8,128)}), f32[432,256]{1,0:T(8,128)}) %reduce-scatter.2.cloned.1.call-update) | async-done | bytes 442384 | tf_op jit(solution)/shard_map/reduce_scatter | solution.py:214
  (8 shorter events, 0.2 us)
Async XLA Ops:
  7.2 13.4 %copy-start.5 = (s32[4,27]{1,0:T(4,128)S(1)}, s32[4,27]{1,0:T(4,128)}, u32[]{:S(2)}) copy-start(s32[4,27]{1,0:T(4,128)} %table.5) | copy-start | bytes 1300
  7.2 120.5 %reduce-scatter.2.cloned.1.call-start = ((), (), s32[]{:S(2)}) async-start(), calls=%async_computation.1 | async-start | bytes 7520256 | tf_op jit(solution)/shard_map/reduce_scatter | solution.py:214
  7.9 0.9 copy-start
  8.8 0.9 copy-start.1
  9.7 0.7 copy-start.2
  10.4 0.7 copy-start.4
  15.1 4.4 %collective-permute-start.1 = (bf16[512,256]{1,0:T(8,128)(2,1)S(1)}, bf16[512,256]{1,0:T(8,128)(2,1)S(1)}, u32[]{:S(2)}, u32[]{:S(2)}) collective-permute-start(bf16[512,256]{1,0:T(8,128)(2,1)S(1)} %get-tuple-element.37), channel_id=1, source_target_pairs={{1,0},{2,1},{3,2},{4,3},{5,4},{6,5},{7,6},{8,7},{9,8},{10,9},{11,1... | collective-permute-start | bytes 786440 | tf_op jit(solution)/shard_map/ppermute | solution.py:180
  16.4 4.2 %collective-permute-start = (bf16[512,256]{1,0:T(8,128)(2,1)S(1)}, bf16[512,256]{1,0:T(8,128)(2,1)S(1)}, u32[]{:S(2)}, u32[]{:S(2)}) collective-permute-start(bf16[512,256]{1,0:T(8,128)(2,1)S(1)} %get-tuple-element.38), channel_id=1, source_target_pairs={{0,1},{1,2},{2,3},{3,4},{4,5},{5,6},{6,7},{7,8},{8,9},{9,10},{10,1... | collective-permute-start | bytes 786440 | tf_op jit(solution)/shard_map/ppermute | solution.py:180
  29.8 11.6 %copy-start.3 = (s32[4,64]{1,0:T(4,128)S(1)}, s32[4,64]{1,0:T(4,128)}, u32[]{:S(2)}) copy-start(s32[4,64]{1,0:T(4,128)} %mask.5) | copy-start | bytes 3076
  29.9 10.4 %collective-permute-start.3 = (bf16[512,256]{1,0:T(8,128)(2,1)S(1)}, bf16[512,256]{1,0:T(8,128)(2,1)S(1)}, u32[]{:S(2)}, u32[]{:S(2)}) collective-permute-start(bf16[512,256]{1,0:T(8,128)(2,1)S(1)} %get-tuple-element.35), channel_id=1, source_target_pairs={{1,0},{2,1},{3,2},{4,3},{5,4},{6,5},{7,6},{8,7},{9,8},{10,9},{11,1... | collective-permute-start | bytes 786440 | tf_op jit(solution)/shard_map/ppermute | solution.py:180
  31.2 10.2 %collective-permute-start.2 = (bf16[512,256]{1,0:T(8,128)(2,1)S(1)}, bf16[512,256]{1,0:T(8,128)(2,1)S(1)}, u32[]{:S(2)}, u32[]{:S(2)}) collective-permute-start(bf16[512,256]{1,0:T(8,128)(2,1)S(1)} %get-tuple-element.36), channel_id=1, source_target_pairs={{0,1},{1,2},{2,3},{3,4},{4,5},{5,6},{6,7},{7,8},{8,9},{9,10},{10,1... | collective-permute-start | bytes 786440 | tf_op jit(solution)/shard_map/ppermute | solution.py:180
Sparse Core Ops, SparseCore 0:
  30.0 97.6 reduce-scatter.1
where the time goes:
time: 135 us
  waiting for transfers between devices  83.7 us (62%)
  Pallas kernels  17.9 us (13%)
  between operations  14.8 us (11%)
  starting transfers between devices  14.7 us (11%)
  local copies, waits for them, and re-layouts  3.25 us (2%)
    reduce_scatter x1, waiting for transfers between devices, on_device(): grad_one = lax.psum_scatter(grad_w, 'gx', scatter_dimension=0, tiled=True)  81.5 us
    ppermute x4, starting transfers between devices, shifted(): lax.ppermute(value, 'gx', [(source, source + steps) for source in range(f...  14.7 us
    pallas_call x1, Pallas kernels, on_device(): pl.pallas_call(second_kernel, out_shape=[rows_of(BF16), rows_of(F32), row...  9.21 us
    pallas_call x1, Pallas kernels, on_device(): pl.pallas_call(third_kernel, out_shape=[rows_of(BF16), rows_of(BF16)], in...  4.69 us
    pallas_call x1, Pallas kernels, on_device(): pl.pallas_call(first_kernel, out_shape=[rows_of(BF16), rows_of(BF16), row...  4.01 us
    unnamed x12, local copies, waits for them, and re-layouts  3.17 us
  transfers between devices with their start and end apart: 5, of which 3 were waited for; matrix products, arithmetic and copies ran while one was open for 0% of the time, Pallas kernels for 3%

commit v1 on v0

--- a/solution.py
+++ b/solution.py
@@ -162,6 +162,98 @@
     total = f_own[...] + f_up[...].astype(F32) + f_low[...].astype(F32)
     grad = (keep * (total + g2[...].astype(F32))).astype(BF16)
     feats_grad[...] = mat(turn, grad).astype(BF16)
+
+
+def peer(z, y, core):
+    return {"gx": z * 4 + y * 2 + core}
+
+
+def remote(source, target, send_sem, recv_sem, device):
+    return pltpu.make_async_remote_copy(
+        src_ref=source, dst_ref=target, send_sem=send_sem, recv_sem=recv_sem,
+        device_id=device, device_id_type=pl.DeviceIdType.MESH,
+    )
+
+
+def reduce_kernel(
+    grad, out, to_core, from_core, to_y, from_y, held, to_z, from_z,
+    core_send, core_recv, y_send, y_recv, z_send, z_recv,
+):
+    me = lax.axis_index("gx")
+    z, y, core = me // 4, (me // 2) % 2, me % 2
+    targets = [(z + 1 + step) % 4 for step in range(4)]
+    partners = [peer(z, y, 1 - core), peer(z, 1 - y, core)]
+    partners += [peer(target, y, core) for target in targets[:3]]
+    barrier = pltpu.get_barrier_semaphore()
+    for device in partners:
+        pl.semaphore_signal(barrier, inc=1, device_id=device, device_id_type=pl.DeviceIdType.MESH)
+    pl.semaphore_wait(barrier, len(partners))
+    by_core, by_y, by_z = [], [], []
+    for step, target in enumerate(targets):
+        for side in range(2):
+            to_core[step, side] = grad[target * 4 + side * 2 + 1 - core].astype(BF16)
+        copy = remote(
+            to_core.at[step], from_core.at[step], core_send.at[step], core_recv.at[step],
+            partners[0],
+        )
+        copy.start()
+        by_core.append(copy)
+    for step, target in enumerate(targets):
+        by_core[step].wait_recv()
+        away = grad[target * 4 + (1 - y) * 2 + core] + from_core[step, 1 - y].astype(F32)
+        to_y[step] = away.astype(BF16)
+        copy = remote(
+            to_y.at[step], from_y.at[step], y_send.at[step], y_recv.at[step], partners[1]
+        )
+        copy.start()
+        by_y.append(copy)
+        held[step] = grad[target * 4 + y * 2 + core] + from_core[step, y].astype(F32)
+    for step in range(3):
+        by_y[step].wait_recv()
+        to_z[step] = (held[step] + from_y[step].astype(F32)).astype(BF16)
+        copy = remote(
+            to_z.at[step], from_z.at[step], z_send.at[step], z_recv.at[step], partners[2 + step]
+        )
+        copy.start()
+        by_z.append(copy)
+    by_y[3].wait_recv()
+    total = held[3] + from_y[3].astype(F32)
+    for step in range(3):
+        by_z[step].wait_recv()
+    out[...] = total + from_z[0].astype(F32) + from_z[1].astype(F32) + from_z[2].astype(F32)
+    for copy in by_core + by_y + by_z:
+        copy.wait_send()
+
+
+def reduce_scattered(grad):
+    devices = lax.axis_size("gx")
+    if devices != 16:
+        return lax.psum_scatter(grad, "gx", scatter_dimension=0, tiled=True)
+    rows, ch = grad.shape
+    share = (rows // devices, ch)
+    return pl.pallas_call(
+        reduce_kernel,
+        out_shape=jax.ShapeDtypeStruct(share, F32),
+        in_specs=[VMEM],
+        out_specs=VMEM,
+        scratch_shapes=[
+            pltpu.VMEM((4, 2, *share), BF16),
+            pltpu.VMEM((4, 2, *share), BF16),
+            pltpu.VMEM((4, *share), BF16),
+            pltpu.VMEM((4, *share), BF16),
+            pltpu.VMEM((4, *share), F32),
+            pltpu.VMEM((3, *share), BF16),
+            pltpu.VMEM((3, *share), BF16),
+            *[pltpu.SemaphoreType.DMA((4,))] * 4,
+            *[pltpu.SemaphoreType.DMA((3,))] * 2,
+        ],
+        cost_estimate=pl.CostEstimate(
+            flops=10**10, bytes_accessed=10**8, transcendentals=0
+        ),
+        compiler_params=pltpu.CompilerParams(
+            vmem_limit_bytes=50 * 2**20, collective_id=0, has_side_effects=True
+        ),
+    )(grad.reshape(devices, *share))
 
 
 def rows_of(kind):
@@ -211,7 +303,7 @@
         scratch_shapes=[WIN, STACK, ACC],
         compiler_params=PARAMS,
     )(x_low, x0, x_up, d_own, d_up, d_low, *small, weight_one)
-    grad_one = lax.psum_scatter(grad_w, "gx", scatter_dimension=0, tiled=True)
+    grad_one = reduce_scattered(grad_w)
     a_low, a_up, f_low, f_up = exchange(a1, f_lower, f_upper)
     block_out, feats_grad = pl.pallas_call(
         third_kernel,

time: 135 us -> 75.1 us (0.56)
  waiting for transfers between devices: 83.7 us -> 1.1 us
  Pallas kernels: 17.9 us -> 53.3 us
  between operations: 14.8 us -> 1.43 us
    reduce_scatter x1 -> x0, waiting for transfers between devices: 81.5 us -> none  [on_device(): grad_one = lax.psum_scatter(grad_w, 'gx', scatter_dimension=0, tiled=True)]
    pallas_call x0 -> x1, Pallas kernels: none -> 35.7 us  [reduce_scattered(): pl.pallas_call(reduce_kernel, out_shape=jax.ShapeDtypeStruct(share, F32),...]
    unnamed x12 -> x11, local copies, waits for them, and re-layouts: 3.17 us -> 3.93 us
  transfers between devices with their start and end apart: 5 -> 4, of which waited for: 3 -> 1; matrix products, arithmetic and copies ran while one was open for 0% -> 0% of each run, Pallas kernels for 3% -> 48%
where the time goes in v1:
time: 75.1 us; the launch traced here: 74.6 us
  Pallas kernels  53.3 us (71%)
  starting transfers between devices  14.7 us (20%)
  local copies, waits for them, and re-layouts  4.01 us (5%)
  between operations  1.43 us (2%)
  waiting for transfers between devices  1.1 us (1%)
    pallas_call x1, Pallas kernels, reduce_scattered(): pl.pallas_call(reduce_kernel, out_shape=jax.ShapeDtypeStruct(share, F32),...  35.7 us
    ppermute x4, starting transfers between devices, shifted(): lax.ppermute(value, 'gx', [(source, source + steps) for source in range(f...  14.7 us
    pallas_call x1, Pallas kernels, on_device(): pl.pallas_call(second_kernel, out_shape=[rows_of(BF16), rows_of(F32), row...  9.21 us
    pallas_call x1, Pallas kernels, on_device(): pl.pallas_call(third_kernel, out_shape=[rows_of(BF16), rows_of(BF16)], in...  4.42 us
    pallas_call x1, Pallas kernels, on_device(): pl.pallas_call(first_kernel, out_shape=[rows_of(BF16), rows_of(BF16), row...  4.02 us
    unnamed x11, local copies, waits for them, and re-layouts  3.93 us
  transfers between devices with their start and end apart: 4, of which 1 were waited for; matrix products, arithmetic and copies ran while one was open for 0% of the time, Pallas kernels for 48%

profile of v1, /device:TPU:0, one launch (start us, length us, event | category | flops | bytes accessed | tf_op | source)
XLA Modules:
  0.0 74.6 jit_solution(1243934743848172538)
XLA Ops:
  0.6 0.0 copy-start.4
  1.3 0.0 copy-start
  1.3 0.9 %copy-done = bf16[4,64,256]{2,1,0:T(8,128)(2,1)S(1)} copy-done((bf16[4,64,256]{2,1,0:T(8,128)(2,1)S(1)}, bf16[4,64,256]{2,1,0:T(8,128)(2,1)}, u32[]{:S(2)}) %copy-start) | copy-done | bytes 131096
  2.2 0.0 copy-start.1
  2.2 0.9 %copy-done.1 = bf16[4,64,256]{2,1,0:T(8,128)(2,1)S(1)} copy-done((bf16[4,64,256]{2,1,0:T(8,128)(2,1)S(1)}, bf16[4,64,256]{2,1,0:T(8,128)(2,1)}, u32[]{:S(2)}) %copy-start.1) | copy-done | bytes 131096
  3.1 0.0 copy-start.2
  3.1 0.7 copy-done.2
  3.8 0.0 copy-start.3
  3.8 0.7 copy-done.3
  4.5 4.0 %shard_map.94 = (bf16[256,256]{1,0:T(8,128)(2,1)S(1)}, bf16[256,256]{1,0:T(8,128)(2,1)S(1)}, f32[256,256]{1,0:T(8,128)S(1)}, bf16[256,256]{1,0:T(8,128)(2,1)S(1)}, bf16[256,256]{1,0:T(8,128)(2,1)S(1)}) custom-call(bf16[256,256]{1,0:T(8,128)(2,1)S(1)} %bitcast.5, bf16[256,256]{1,0:T(8,128)(2,1)S(1)} %bitcast.6, s32[4,64]{1,0:T(4,128)S(1)} %copy-done.2, ...), custom_call_target="tpu_custom_call" | custom-call | tf_op jit(solution)/shard_map/pallas_call | solution.py:286
  8.5 1.3 %collective-permute-start.1 = (bf16[512,256]{1,0:T(8,128)(2,1)S(1)}, bf16[512,256]{1,0:T(8,128)(2,1)S(1)}, u32[]{:S(2)}, u32[]{:S(2)}) collective-permute-start(bf16[512,256]{1,0:T(8,128)(2,1)S(1)} %get-tuple-element.37), channel_id=1, source_target_pairs={{1,0},{2,1},{3,2},{4,3},{5,4},{6,5},{7,6},{8,7},{9,8},{10,9},{11,1... | collective-permute-start | bytes 786440 | tf_op jit(solution)/shard_map/ppermute | solution.py:272
  9.8 3.0 %collective-permute-start = (bf16[512,256]{1,0:T(8,128)(2,1)S(1)}, bf16[512,256]{1,0:T(8,128)(2,1)S(1)}, u32[]{:S(2)}, u32[]{:S(2)}) collective-permute-start(bf16[512,256]{1,0:T(8,128)(2,1)S(1)} %get-tuple-element.38), channel_id=1, source_target_pairs={{0,1},{1,2},{2,3},{3,4},{4,5},{5,6},{6,7},{7,8},{8,9},{9,10},{10,1... | collective-permute-start | bytes 786440 | tf_op jit(solution)/shard_map/ppermute | solution.py:272
  12.9 0.0 collective-permute-done.1
  12.9 1.1 %collective-permute-done = bf16[512,256]{1,0:T(8,128)(2,1)S(1)} collective-permute-done((bf16[512,256]{1,0:T(8,128)(2,1)S(1)}, bf16[512,256]{1,0:T(8,128)(2,1)S(1)}, u32[]{:S(2)}, u32[]{:S(2)}) %collective-permute-start) | collective-permute-done | bytes 262176 | tf_op jit(solution)/shard_map/ppermute | solution.py:272
  14.0 0.0 copy-done.4
  14.1 9.2 %shard_map.95 = (bf16[256,256]{1,0:T(8,128)(2,1)S(1)}, f32[256,256]{1,0:T(8,128)S(1)}, bf16[256,256]{1,0:T(8,128)(2,1)S(1)}, bf16[256,256]{1,0:T(8,128)(2,1)S(1)}, f32[6912,256]{1,0:T(8,128)}) custom-call(bf16[256,256]{1,0:T(8,128)(2,1)S(1)} %get-tuple-element.32.x0_low, bf16[256,256]{1,0:T(8,128)(2,1)S(1)} %get-tuple-element.15.x0, ...), custom_call_target="tpu_custom_call" | custom-call | tf_op jit(solution)/shard_map/pallas_call | solution.py:295
  23.3 1.3 %collective-permute-start.3 = (bf16[512,256]{1,0:T(8,128)(2,1)S(1)}, bf16[512,256]{1,0:T(8,128)(2,1)S(1)}, u32[]{:S(2)}, u32[]{:S(2)}) collective-permute-start(bf16[512,256]{1,0:T(8,128)(2,1)S(1)} %get-tuple-element.35), channel_id=1, source_target_pairs={{1,0},{2,1},{3,2},{4,3},{5,4},{6,5},{7,6},{8,7},{9,8},{10,9},{11,1... | collective-permute-start | bytes 786440 | tf_op jit(solution)/shard_map/ppermute | solution.py:272
  24.6 9.1 %collective-permute-start.2 = (bf16[512,256]{1,0:T(8,128)(2,1)S(1)}, bf16[512,256]{1,0:T(8,128)(2,1)S(1)}, u32[]{:S(2)}, u32[]{:S(2)}) collective-permute-start(bf16[512,256]{1,0:T(8,128)(2,1)S(1)} %get-tuple-element.36), channel_id=1, source_target_pairs={{0,1},{1,2},{2,3},{3,4},{4,5},{5,6},{6,7},{7,8},{8,9},{9,10},{10,1... | collective-permute-start | bytes 786440 | tf_op jit(solution)/shard_map/ppermute | solution.py:272
  33.7 35.7 %shard_map.97 = f32[432,256]{1,0:T(8,128)S(1)} custom-call(f32[16,432,256]{2,1,0:T(8,128)} %bitcast.7), custom_call_target="tpu_custom_call" | custom-call | flops 10000000000 | bytes 100000000 | tf_op jit(solution)/shard_map/pallas_call | solution.py:234
  69.4 0.0 collective-permute-done.3
  69.4 0.0 collective-permute-done.2
  69.5 4.4 %shard_map.96 = (bf16[256,256]{1,0:T(8,128)(2,1)}, bf16[256,256]{1,0:T(8,128)(2,1)}) custom-call(bf16[256,256]{1,0:T(8,128)(2,1)S(1)} %get-tuple-element.28.a_low, bf16[256,256]{1,0:T(8,128)(2,1)S(1)} %get-tuple-element.19.a1, bf16[256,256]{1,0:T(8,128)(2,1)S(1)} %get-tuple-element.30.a_up, f32[256,256]{1,0:T(8,128)S(1)} %get-tuple-element.22.f_own, ...), custom_call_target="tpu_custom_call" | custom-call | tf_op jit(solution)/shard_map/pallas_call | solution.py:308
  73.9 0.8 %copy.12 = f32[432,256]{1,0:T(8,128)} copy(f32[432,256]{1,0:T(8,128)S(1)} %shard_map.97) | data formatting | bytes 884736
  (6 shorter events, 0.1 us)
Async XLA Ops:
  0.6 13.4 %copy-start.4 = (s32[4,27]{1,0:T(4,128)S(1)}, s32[4,27]{1,0:T(4,128)}, u32[]{:S(2)}) copy-start(s32[4,27]{1,0:T(4,128)} %table.5) | copy-start | bytes 1300
  1.3 0.9 %copy-start = (bf16[4,64,256]{2,1,0:T(8,128)(2,1)S(1)}, bf16[4,64,256]{2,1,0:T(8,128)(2,1)}, u32[]{:S(2)}) copy-start(bf16[4,64,256]{2,1,0:T(8,128)(2,1)} %param.7) | copy-start | bytes 393220
  2.2 0.9 %copy-start.1 = (bf16[4,64,256]{2,1,0:T(8,128)(2,1)S(1)}, bf16[4,64,256]{2,1,0:T(8,128)(2,1)}, u32[]{:S(2)}) copy-start(bf16[4,64,256]{2,1,0:T(8,128)(2,1)} %param.13) | copy-start | bytes 393220
  3.1 0.7 copy-start.2
  3.8 0.7 copy-start.3
  8.5 4.4 %collective-permute-start.1 = (bf16[512,256]{1,0:T(8,128)(2,1)S(1)}, bf16[512,256]{1,0:T(8,128)(2,1)S(1)}, u32[]{:S(2)}, u32[]{:S(2)}) collective-permute-start(bf16[512,256]{1,0:T(8,128)(2,1)S(1)} %get-tuple-element.37), channel_id=1, source_target_pairs={{1,0},{2,1},{3,2},{4,3},{5,4},{6,5},{7,6},{8,7},{9,8},{10,9},{11,1... | collective-permute-start | bytes 786440 | tf_op jit(solution)/shard_map/ppermute | solution.py:272
  9.8 4.2 %collective-permute-start = (bf16[512,256]{1,0:T(8,128)(2,1)S(1)}, bf16[512,256]{1,0:T(8,128)(2,1)S(1)}, u32[]{:S(2)}, u32[]{:S(2)}) collective-permute-start(bf16[512,256]{1,0:T(8,128)(2,1)S(1)} %get-tuple-element.38), channel_id=1, source_target_pairs={{0,1},{1,2},{2,3},{3,4},{4,5},{5,6},{6,7},{7,8},{8,9},{9,10},{10,1... | collective-permute-start | bytes 786440 | tf_op jit(solution)/shard_map/ppermute | solution.py:272
  23.3 46.1 %collective-permute-start.3 = (bf16[512,256]{1,0:T(8,128)(2,1)S(1)}, bf16[512,256]{1,0:T(8,128)(2,1)S(1)}, u32[]{:S(2)}, u32[]{:S(2)}) collective-permute-start(bf16[512,256]{1,0:T(8,128)(2,1)S(1)} %get-tuple-element.35), channel_id=1, source_target_pairs={{1,0},{2,1},{3,2},{4,3},{5,4},{6,5},{7,6},{8,7},{9,8},{10,9},{11,1... | collective-permute-start | bytes 786440 | tf_op jit(solution)/shard_map/ppermute | solution.py:272
  24.6 44.8 %collective-permute-start.2 = (bf16[512,256]{1,0:T(8,128)(2,1)S(1)}, bf16[512,256]{1,0:T(8,128)(2,1)S(1)}, u32[]{:S(2)}, u32[]{:S(2)}) collective-permute-start(bf16[512,256]{1,0:T(8,128)(2,1)S(1)} %get-tuple-element.36), channel_id=1, source_target_pairs={{0,1},{1,2},{2,3},{3,4},{4,5},{5,6},{6,7},{7,8},{8,9},{9,10},{10,1... | collective-permute-start | bytes 786440 | tf_op jit(solution)/shard_map/ppermute | solution.py:272

commit v2 on v0

--- a/solution.py
+++ b/solution.py
@@ -164,6 +164,17 @@
     feats_grad[...] = mat(turn, grad).astype(BF16)
 
 
+def peer(z, y, core):
+    return {"gx": z * 4 + y * 2 + core}
+
+
+def remote(source, target, send_sem, recv_sem, device):
+    return pltpu.make_async_remote_copy(
+        src_ref=source, dst_ref=target, send_sem=send_sem, recv_sem=recv_sem,
+        device_id=device, device_id_type=pl.DeviceIdType.MESH,
+    )
+
+
 def rows_of(kind):
     return jax.ShapeDtypeStruct((ROWS, 256), kind)
 
@@ -186,7 +197,200 @@
     return up[:ROWS], down[:ROWS], up[ROWS:], down[ROWS:]
 
 
+def whole_kernel(
+    feats, cot, mask, table, counts, w1_hbm, w2_hbm,
+    block_out, feats_grad, grad_out,
+    w1, w2, win, stack, acc, g2, own, grad, field, from_low, from_up, down_sum, up_sum,
+    sum_low, sum_up, to_core, from_core, to_y, from_y, held, to_z, from_z,
+    load, ring_send, ring_recv, sum_send, sum_recv,
+    core_send, core_recv, y_send, y_recv, z_send, z_recv,
+):
+    me, devices, share = lax.axis_index("gx"), lax.axis_size("gx"), grad_out.shape[0]
+    z, y, core = me // 4, (me // 2) % 2, me % 2
+    targets = [(z + 1 + step) % 4 for step in range(4)]
+    partners = [peer(z, y, 1 - core), peer(z, 1 - y, core)]
+    partners += [peer(target, y, core) for target in targets[:3]]
+    other = {"gx": (me + 2 * core - 1 + devices) % devices}
+    above, below = {"gx": (me + 1) % devices}, {"gx": (me - 1 + devices) % devices}
+    barrier = pltpu.get_barrier_semaphore()
+    for device in [*partners, other]:
+        pl.semaphore_signal(barrier, inc=1, device_id=device, device_id_type=pl.DeviceIdType.MESH)
+    load_w2 = pltpu.make_async_copy(w2_hbm, w2, load.at[0])
+    load_w1 = pltpu.make_async_copy(w1_hbm, w1, load.at[1])
+    load_w2.start()
+    load_w1.start()
+    has_above, has_below = me < devices - 1, me > 0
+
+    @pl.when(me == 0)
+    def _():
+        from_low[...] = jnp.zeros(from_low.shape, BF16)
+        sum_low[...] = jnp.zeros(sum_low.shape, BF16)
+
+    @pl.when(me == devices - 1)
+    def _():
+        from_up[...] = jnp.zeros(from_up.shape, BF16)
+        sum_up[...] = jnp.zeros(sum_up.shape, BF16)
+
+    def ring(n, up_source, low_slot, down_source, up_slot, send, recv):
+        return (
+            remote(up_source.at[n], low_slot.at[n], send.at[n, 0], recv.at[n, 0], above),
+            remote(down_source.at[n], up_slot.at[n], send.at[n, 1], recv.at[n, 1], below),
+        )
+
+    def start(pair):
+        pl.when(has_above)(pair[0].start)
+        pl.when(has_below)(pair[1].start)
+
+    def wait_recv(pair):
+        pl.when(has_below)(pair[0].wait_recv)
+        pl.when(has_above)(pair[1].wait_recv)
+
+    def wait_send(pair):
+        pl.when(has_above)(pair[0].wait_send)
+        pl.when(has_below)(pair[1].wait_send)
+
+    fields = [ring(n, field, from_low, field, from_up, ring_send, ring_recv) for n in range(2)]
+    sums = [ring(n, up_sum, sum_low, down_sum, sum_up, sum_send, sum_recv) for n in range(2)]
+
+    keep = mask_rows(mask, counts)
+    turn = to_rows()
+    field[0] = (mat(turn, feats[...]) * keep).astype(BF16)
+    pl.semaphore_wait(barrier, len(partners) + 1)
+    start(fields[0])
+    g2[...] = (mat(turn, cot[...]) * keep).astype(BF16)
+    picks = pickers(table)
+    load_w2.wait()
+    spread_back(picks, g2[...], w2, acc, own, down_sum.at[0], up_sum.at[0])
+    start(sums[0])
+    load_w1.wait()
+    wait_recv(fields[0])
+    gather_windows(picks, from_low.at[0], field.at[0], from_up.at[0], win)
+    build_stack(win, stack)
+    y1 = mat(stack[...], w1[...]) * keep
+    sig = 1.0 / (1.0 + jnp.exp(-y1))
+    field[1] = (y1 * sig).astype(BF16)
+    start(fields[1])
+    wait_recv(sums[0])
+    da1 = own[...] + sum_up[0].astype(F32) + sum_low[0].astype(F32)
+    g1 = (da1 * keep * (sig * (1.0 + y1 * (1.0 - sig)))).astype(BF16)
+    for o in range(27):
+        at = slice(o * 256, (o + 1) * 256)
+        grad[at, :] = lax.dot_general(
+            stack[:, at], g1, (((0,), (0,)), ((), ())), preferred_element_type=F32
+        )
+
+    def part(target, side, half):
+        first = pl.multiple_of((target * 4 + side * 2 + half) * share, 16)
+        return grad[pl.ds(first, share), :]
+
+    by_core, by_y, by_z = [], [], []
+    for step, target in enumerate(targets):
+        for side in range(2):
+            to_core[step, side] = part(target, side, 1 - core).astype(BF16)
+        copy = remote(
+            to_core.at[step], from_core.at[step], core_send.at[step], core_recv.at[step],
+            partners[0],
+        )
+        copy.start()
+        by_core.append(copy)
+
+    def core_to_y(step):
+        by_core[step].wait_recv()
+        target = targets[step]
+        away = part(target, 1 - y, core) + from_core[step, 1 - y].astype(F32)
+        to_y[step] = away.astype(BF16)
+        copy = remote(
+            to_y.at[step], from_y.at[step], y_send.at[step], y_recv.at[step], partners[1]
+        )
+        copy.start()
+        by_y.append(copy)
+        held[step] = part(target, y, core) + from_core[step, y].astype(F32)
+
+    def y_to_z(step):
+        by_y[step].wait_recv()
+        to_z[step] = (held[step] + from_y[step].astype(F32)).astype(BF16)
+        copy = remote(
+            to_z.at[step], from_z.at[step], z_send.at[step], z_recv.at[step], partners[2 + step]
+        )
+        copy.start()
+        by_z.append(copy)
+
+    core_to_y(0)
+    core_to_y(1)
+    spread_back(picks, g1, w1, acc, own, down_sum.at[1], up_sum.at[1])
+    start(sums[1])
+    core_to_y(2)
+    core_to_y(3)
+    y_to_z(0)
+    wait_recv(fields[1])
+    gather_windows(picks, from_low.at[1], field.at[1], from_up.at[1], win)
+    build_stack(win, stack)
+    y_to_z(1)
+    y2 = mat(stack[...], w2[...]) * keep
+    out = (y2 + field[0].astype(F32)).astype(BF16)
+    turn = from_rows()
+    block_out[...] = mat(turn, out).astype(BF16)
+    y_to_z(2)
+    wait_recv(sums[1])
+    total = own[...] + sum_up[1].astype(F32) + sum_low[1].astype(F32)
+    back = (keep * (total + g2[...].astype(F32))).astype(BF16)
+    feats_grad[...] = mat(turn, back).astype(BF16)
+    by_y[3].wait_recv()
+    grad_out[...] = held[3] + from_y[3].astype(F32)
+    for step in range(3):
+        by_z[step].wait_recv()
+        grad_out[...] += from_z[step].astype(F32)
+    for copy in by_core + by_y + by_z:
+        copy.wait_send()
+    for pair in fields + sums:
+        wait_send(pair)
+
+
+def in_one(feats, voxel_mask, brick_table, counts, weight_one, weight_two, cotangent):
+    per, vb, ch = feats.shape
+    share = (weight_one.shape[0] // lax.axis_size("gx"), ch)
+    anywhere = pl.BlockSpec(memory_space=pl.ANY)
+    pair = pltpu.VMEM((2, ROWS, ch), BF16)
+    block_out, feats_grad, grad_one = pl.pallas_call(
+        whole_kernel,
+        out_shape=[rows_of(BF16), rows_of(BF16), jax.ShapeDtypeStruct(share, F32)],
+        in_specs=[VMEM, VMEM, VMEM, VMEM, SMEM, anywhere, anywhere],
+        out_specs=[VMEM] * 3,
+        scratch_shapes=[
+            pltpu.VMEM(weight_one.shape, BF16),
+            pltpu.VMEM(weight_two.shape, BF16),
+            WIN,
+            STACK,
+            ACC,
+            pltpu.VMEM((ROWS, ch), BF16),
+            pltpu.VMEM((ROWS, ch), F32),
+            pltpu.VMEM(weight_one.shape, F32),
+            *[pair] * 7,
+            pltpu.VMEM((4, 2, *share), BF16),
+            pltpu.VMEM((4, 2, *share), BF16),
+            pltpu.VMEM((4, *share), BF16),
+            pltpu.VMEM((4, *share), BF16),
+            pltpu.VMEM((4, *share), F32),
+            pltpu.VMEM((3, *share), BF16),
+            pltpu.VMEM((3, *share), BF16),
+            pltpu.SemaphoreType.DMA((2,)),
+            *[pltpu.SemaphoreType.DMA((2, 2))] * 4,
+            *[pltpu.SemaphoreType.DMA((4,))] * 4,
+            *[pltpu.SemaphoreType.DMA((3,))] * 2,
+        ],
+        compiler_params=pltpu.CompilerParams(
+            vmem_limit_bytes=56 * 2**20, collective_id=0, has_side_effects=True
+        ),
+    )(
+        feats.reshape(per * vb, ch), cotangent.reshape(per * vb, ch), voxel_mask, brick_table,
+        counts, weight_one, weight_two,
+    )
+    return (block_out.reshape(per, vb, ch), feats_grad.reshape(per, vb, ch), grad_one)
+
+
 def on_device(feats, voxel_mask, brick_table, counts, weight_one, weight_two, cotangent):
+    if lax.axis_size("gx") == 16:
+        return in_one(feats, voxel_mask, brick_table, counts, weight_one, weight_two, cotangent)
     per, vb, ch = feats.shape
     kc = weight_one.shape[0]
     small = (voxel_mask, brick_table, counts)

time: 135 us -> 52.9 us (0.39)
  waiting for transfers between devices: 83.7 us -> 0 us
  Pallas kernels: 17.9 us -> 46.5 us
  starting transfers between devices: 14.7 us -> 0 us
  between operations: 14.8 us -> 1.29 us
  local copies, waits for them, and re-layouts: 3.25 us -> 4.94 us
    reduce_scatter x1 -> x0, waiting for transfers between devices: 81.5 us -> none  [on_device(): grad_one = lax.psum_scatter(grad_w, 'gx', scatter_dimension=0, tiled=True)]
    pallas_call x3 -> x1, Pallas kernels: 17.9 us -> 46.5 us  [in_one(): pl.pallas_call(whole_kernel, out_shape=[rows_of(BF16), rows_of(BF16), jax...]
    ppermute x4 -> x0, starting transfers between devices: 14.7 us -> none  [shifted(): lax.ppermute(value, 'gx', [(source, source + steps) for source in range(f...]
    ppermute x4 -> x0, waiting for transfers between devices: 2.19 us -> none  [shifted(): lax.ppermute(value, 'gx', [(source, source + steps) for source in range(f...]
    unnamed x12 -> x3, local copies, waits for them, and re-layouts: 3.17 us -> 4.94 us
  transfers between devices with their start and end apart: 5 -> 0, of which waited for: 3 -> 0; matrix products, arithmetic and copies ran while one was open for 0% -> 0% of each run, Pallas kernels for 3% -> 0%
where the time goes in v2:
time: 52.9 us; the launch traced here: 52.7 us
  Pallas kernels  46.5 us (88%)
  local copies, waits for them, and re-layouts  4.94 us (9%)
  between operations  1.29 us (2%)
    pallas_call x1, Pallas kernels, in_one(): pl.pallas_call(whole_kernel, out_shape=[rows_of(BF16), rows_of(BF16), jax...  46.5 us
    unnamed x3, local copies, waits for them, and re-layouts  4.94 us

profile of v2, /device:TPU:0, one launch (start us, length us, event | category | flops | bytes accessed | tf_op | source)
XLA Modules:
  0.0 52.7 jit_solution(12612018769993929131)
XLA Ops:
  1.3 46.5 %shard_map.94 = (bf16[256,256]{1,0:T(8,128)(2,1)}, bf16[256,256]{1,0:T(8,128)(2,1)}, f32[432,256]{1,0:T(8,128)}) custom-call(bf16[256,256]{1,0:T(8,128)(2,1)} %bitcast.4, bf16[256,256]{1,0:T(8,128)(2,1)} %bitcast.5, s32[4,64]{1,0:T(4,128)} %mask.1, s32[4,27]{1,0:T(4,128)} %table.1, s32[1]{0:T(128)S(6)} %copy.13.counts, bf16[6912,256]{1,0:T(8,128)(2,1)} %w1_hbm.1, ...), custom_call_target="tpu_custom_call" | custom-call | tf_op jit(solution)/shard_map/pallas_call | solution.py:354
  47.8 1.6 %copy.14 = bf16[4,64,256]{2,1,0:T(8,128)(2,1)} copy(bf16[4,64,256]{2,1,0:T(8,128)(2,1)} %bitcast.7) | data formatting | bytes 262144
  49.3 1.6 %copy.15 = bf16[4,64,256]{2,1,0:T(8,128)(2,1)} copy(bf16[4,64,256]{2,1,0:T(8,128)(2,1)} %bitcast.6) | data formatting | bytes 262144
  50.9 1.8 %copy.16 = f32[432,256]{1,0:T(8,128)} copy(f32[432,256]{1,0:T(8,128)} %get-tuple-element.14) | data formatting | bytes 884736

commit v3 on v2

--- a/solution.py
+++ b/solution.py
@@ -273,20 +273,25 @@
     wait_recv(sums[0])
     da1 = own[...] + sum_up[0].astype(F32) + sum_low[0].astype(F32)
     g1 = (da1 * keep * (sig * (1.0 + y1 * (1.0 - sig)))).astype(BF16)
-    for o in range(27):
-        at = slice(o * 256, (o + 1) * 256)
-        grad[at, :] = lax.dot_general(
-            stack[:, at], g1, (((0,), (0,)), ((), ())), preferred_element_type=F32
-        )
-
-    def part(target, side, half):
-        first = pl.multiple_of((target * 4 + side * 2 + half) * share, 16)
-        return grad[pl.ds(first, share), :]
+    half = share // 32 * 16
+    pieces = [(0, half), (half, share - half)]
+
+    def part(target, side, lane, first, size):
+        start_row = (target * 4 + side * 2 + lane) * share + first
+        return grad[pl.ds(pl.multiple_of(start_row, 16), size), :]
 
     by_core, by_y, by_z = [], [], []
-    for step, target in enumerate(targets):
+
+    def grad_to_core(step):
+        target = targets[step]
+        first = target * 27 // 4 - target // 3
+        for n in range(8):
+            at = pl.ds(pl.multiple_of((first + n) * 256, 256), 256)
+            grad[at, :] = lax.dot_general(
+                stack[:, at], g1, (((0,), (0,)), ((), ())), preferred_element_type=F32
+            )
         for side in range(2):
-            to_core[step, side] = part(target, side, 1 - core).astype(BF16)
+            to_core[step, side] = part(target, side, 1 - core, 0, share).astype(BF16)
         copy = remote(
             to_core.at[step], from_core.at[step], core_send.at[step], core_recv.at[step],
             partners[0],
@@ -297,48 +302,59 @@
     def core_to_y(step):
         by_core[step].wait_recv()
         target = targets[step]
-        away = part(target, 1 - y, core) + from_core[step, 1 - y].astype(F32)
-        to_y[step] = away.astype(BF16)
+        for n, (first, size) in enumerate(pieces):
+            at = pl.ds(first, size)
+            away = part(target, 1 - y, core, first, size)
+            to_y[step, at] = (away + from_core[step, 1 - y, at].astype(F32)).astype(BF16)
+            copy = remote(
+                to_y.at[step, at], from_y.at[step, at], y_send.at[step, n], y_recv.at[step, n],
+                partners[1],
+            )
+            copy.start()
+            by_y.append(copy)
+        held[step] = part(target, y, core, 0, share) + from_core[step, y].astype(F32)
+
+    def y_to_z(step, n):
+        by_y[2 * step + n].wait_recv()
+        at = pl.ds(*pieces[n])
+        to_z[step, at] = (held[step, at] + from_y[step, at].astype(F32)).astype(BF16)
         copy = remote(
-            to_y.at[step], from_y.at[step], y_send.at[step], y_recv.at[step], partners[1]
-        )
-        copy.start()
-        by_y.append(copy)
-        held[step] = part(target, y, core) + from_core[step, y].astype(F32)
-
-    def y_to_z(step):
-        by_y[step].wait_recv()
-        to_z[step] = (held[step] + from_y[step].astype(F32)).astype(BF16)
-        copy = remote(
-            to_z.at[step], from_z.at[step], z_send.at[step], z_recv.at[step], partners[2 + step]
+            to_z.at[step, at], from_z.at[step, at], z_send.at[step, n], z_recv.at[step, n],
+            partners[2 + step],
         )
         copy.start()
         by_z.append(copy)
 
+    grad_to_core(0)
+    grad_to_core(1)
     core_to_y(0)
+    grad_to_core(2)
     core_to_y(1)
-    spread_back(picks, g1, w1, acc, own, down_sum.at[1], up_sum.at[1])
-    start(sums[1])
+    grad_to_core(3)
     core_to_y(2)
     core_to_y(3)
-    y_to_z(0)
+    y_to_z(0, 0)
+    spread_back(picks, g1, w1, acc, own, down_sum.at[1], up_sum.at[1])
+    y_to_z(0, 1)
+    start(sums[1])
     wait_recv(fields[1])
     gather_windows(picks, from_low.at[1], field.at[1], from_up.at[1], win)
     build_stack(win, stack)
-    y_to_z(1)
+    y_to_z(1, 0)
     y2 = mat(stack[...], w2[...]) * keep
-    out = (y2 + field[0].astype(F32)).astype(BF16)
-    turn = from_rows()
-    block_out[...] = mat(turn, out).astype(BF16)
-    y_to_z(2)
+    block_out[...] = (y2 + field[0].astype(F32)).astype(BF16)
+    y_to_z(1, 1)
+    y_to_z(2, 0)
+    y_to_z(2, 1)
     wait_recv(sums[1])
     total = own[...] + sum_up[1].astype(F32) + sum_low[1].astype(F32)
-    back = (keep * (total + g2[...].astype(F32))).astype(BF16)
-    feats_grad[...] = mat(turn, back).astype(BF16)
-    by_y[3].wait_recv()
+    feats_grad[...] = (keep * (total + g2[...].astype(F32))).astype(BF16)
+    by_y[6].wait_recv()
+    by_y[7].wait_recv()
     grad_out[...] = held[3] + from_y[3].astype(F32)
     for step in range(3):
-        by_z[step].wait_recv()
+        by_z[2 * step].wait_recv()
+        by_z[2 * step + 1].wait_recv()
         grad_out[...] += from_z[step].astype(F32)
     for copy in by_core + by_y + by_z:
         copy.wait_send()
@@ -346,14 +362,22 @@
         wait_send(pair)
 
 
+def last_kernel(block_rows, grad_rows, share, block_out, feats_grad, grad_out):
+    turn = from_rows()
+    block_out[...] = mat(turn, block_rows[...]).astype(BF16)
+    feats_grad[...] = mat(turn, grad_rows[...]).astype(BF16)
+    grad_out[...] = share[...]
+
+
 def in_one(feats, voxel_mask, brick_table, counts, weight_one, weight_two, cotangent):
     per, vb, ch = feats.shape
     share = (weight_one.shape[0] // lax.axis_size("gx"), ch)
     anywhere = pl.BlockSpec(memory_space=pl.ANY)
     pair = pltpu.VMEM((2, ROWS, ch), BF16)
-    block_out, feats_grad, grad_one = pl.pallas_call(
+    shapes = [rows_of(BF16), rows_of(BF16), jax.ShapeDtypeStruct(share, F32)]
+    parts = pl.pallas_call(
         whole_kernel,
-        out_shape=[rows_of(BF16), rows_of(BF16), jax.ShapeDtypeStruct(share, F32)],
+        out_shape=shapes,
         in_specs=[VMEM, VMEM, VMEM, VMEM, SMEM, anywhere, anywhere],
         out_specs=[VMEM] * 3,
         scratch_shapes=[
@@ -375,8 +399,9 @@
             pltpu.VMEM((3, *share), BF16),
             pltpu.SemaphoreType.DMA((2,)),
             *[pltpu.SemaphoreType.DMA((2, 2))] * 4,
-            *[pltpu.SemaphoreType.DMA((4,))] * 4,
-            *[pltpu.SemaphoreType.DMA((3,))] * 2,
+            *[pltpu.SemaphoreType.DMA((4,))] * 2,
+            *[pltpu.SemaphoreType.DMA((4, 2))] * 2,
+            *[pltpu.SemaphoreType.DMA((3, 2))] * 2,
         ],
         compiler_params=pltpu.CompilerParams(
             vmem_limit_bytes=56 * 2**20, collective_id=0, has_side_effects=True
@@ -385,6 +410,10 @@
         feats.reshape(per * vb, ch), cotangent.reshape(per * vb, ch), voxel_mask, brick_table,
         counts, weight_one, weight_two,
     )
+    block_out, feats_grad, grad_one = pl.pallas_call(
+        last_kernel, out_shape=shapes, in_specs=[VMEM] * 3, out_specs=[VMEM] * 3,
+        compiler_params=pltpu.CompilerParams(vmem_limit_bytes=60 * 2**20),
+    )(*parts)
     return (block_out.reshape(per, vb, ch), feats_grad.reshape(per, vb, ch), grad_one)
 
 

time: 52.9 us -> 46.2 us (0.87)
  local copies, waits for them, and re-layouts: 4.94 us -> 0 us
  Pallas kernels: 46.5 us -> 44.7 us
    unnamed x3 -> x0, local copies, waits for them, and re-layouts: 4.94 us -> none
    pallas_call x1 -> x2, Pallas kernels: 46.5 us -> 44.7 us  [the longest x1 42.5 us: in_one(): pl.pallas_call(whole_kernel, out_shape=shapes, in_specs=[VMEM, VMEM, VMEM...]
where the time goes in v3:
time: 46.2 us; the launch traced here: 46 us
  Pallas kernels  44.7 us (97%)
  between operations  1.29 us (3%)
    pallas_call x1, Pallas kernels, in_one(): pl.pallas_call(whole_kernel, out_shape=shapes, in_specs=[VMEM, VMEM, VMEM...  42.5 us
    pallas_call x1, Pallas kernels, in_one(): pl.pallas_call(last_kernel, out_shape=shapes, in_specs=[VMEM] * 3, out_sp...  2.23 us

profile of v3, /device:TPU:0, one launch (start us, length us, event | category | flops | bytes accessed | tf_op | source)
XLA Modules:
  0.0 46.0 jit_solution(16246584866396147220)
XLA Ops:
  1.3 42.5 %shard_map.94 = (bf16[256,256]{1,0:T(8,128)(2,1)}, bf16[256,256]{1,0:T(8,128)(2,1)}, f32[432,256]{1,0:T(8,128)}) custom-call(bf16[256,256]{1,0:T(8,128)(2,1)} %bitcast.4, bf16[256,256]{1,0:T(8,128)(2,1)} %bitcast.5, s32[4,64]{1,0:T(4,128)} %mask.1, s32[4,27]{1,0:T(4,128)} %table.1, s32[1]{0:T(128)S(6)} %copy.10.counts, bf16[6912,256]{1,0:T(8,128)(2,1)} %w1_hbm.1, ...), custom_call_target="tpu_custom_call" | custom-call | tf_op jit(solution)/shard_map/pallas_call | solution.py:378
  43.8 2.2 %shard_map.95 = (bf16[256,256]{1,0:T(8,128)(2,1)}, bf16[256,256]{1,0:T(8,128)(2,1)}, f32[432,256]{1,0:T(8,128)}) custom-call(bf16[256,256]{1,0:T(8,128)(2,1)} %get-tuple-element.9.block_rows, bf16[256,256]{1,0:T(8,128)(2,1)} %get-tuple-element.10.grad_rows, f32[432,256]{1,0:T(8,128)} %get-tuple-element.11.share), custom_call_target="tpu_custom_call" | custom-call | tf_op jit(solution)/shard_map/pallas_call | solution.py:413

commit v4 on v3

--- a/solution.py
+++ b/solution.py
@@ -207,7 +207,7 @@
 ):
     me, devices, share = lax.axis_index("gx"), lax.axis_size("gx"), grad_out.shape[0]
     z, y, core = me // 4, (me // 2) % 2, me % 2
-    targets = [(z + 1 + step) % 4 for step in range(4)]
+    targets = [3 - z, (z + 2) % 4, z + 1 - 2 * (z % 2), z]
     partners = [peer(z, y, 1 - core), peer(z, 1 - y, core)]
     partners += [peer(target, y, core) for target in targets[:3]]
     other = {"gx": (me + 2 * core - 1 + devices) % devices}

time: 46.2 us -> 47.1 us (1.019)
  Pallas kernels: 44.7 us -> 45.7 us
    pallas_call x1, Pallas kernels: 42.5 us -> 43.4 us  [in_one(): pl.pallas_call(whole_kernel, out_shape=shapes, in_specs=[VMEM, VMEM, VMEM...]
where the time goes in v4:
time: 47.1 us; the launch traced here: 46.9 us
  Pallas kernels  45.7 us (97%)
  between operations  1.29 us (3%)
    pallas_call x1, Pallas kernels, in_one(): pl.pallas_call(whole_kernel, out_shape=shapes, in_specs=[VMEM, VMEM, VMEM...  43.4 us
    pallas_call x1, Pallas kernels, in_one(): pl.pallas_call(last_kernel, out_shape=shapes, in_specs=[VMEM] * 3, out_sp...  2.23 us

profile of v4, /device:TPU:0, one launch (start us, length us, event | category | flops | bytes accessed | tf_op | source)
XLA Modules:
  0.0 46.9 jit_solution(6470152847354782718)
XLA Ops:
  1.3 43.4 %shard_map.94 = (bf16[256,256]{1,0:T(8,128)(2,1)}, bf16[256,256]{1,0:T(8,128)(2,1)}, f32[432,256]{1,0:T(8,128)}) custom-call(bf16[256,256]{1,0:T(8,128)(2,1)} %bitcast.4, bf16[256,256]{1,0:T(8,128)(2,1)} %bitcast.5, s32[4,64]{1,0:T(4,128)} %mask.1, s32[4,27]{1,0:T(4,128)} %table.1, s32[1]{0:T(128)S(6)} %copy.10.counts, bf16[6912,256]{1,0:T(8,128)(2,1)} %w1_hbm.1, ...), custom_call_target="tpu_custom_call" | custom-call | tf_op jit(solution)/shard_map/pallas_call | solution.py:378
  44.7 2.2 %shard_map.95 = (bf16[256,256]{1,0:T(8,128)(2,1)}, bf16[256,256]{1,0:T(8,128)(2,1)}, f32[432,256]{1,0:T(8,128)}) custom-call(bf16[256,256]{1,0:T(8,128)(2,1)} %get-tuple-element.9.block_rows, bf16[256,256]{1,0:T(8,128)(2,1)} %get-tuple-element.10.grad_rows, f32[432,256]{1,0:T(8,128)} %get-tuple-element.11.share), custom_call_target="tpu_custom_call" | custom-call | tf_op jit(solution)/shard_map/pallas_call | solution.py:413
